TPU v7x, 256 devices: a whole 4x4x8 slice. The times are simulated.
256 devices in a mesh: lon: 64 (over z, y_lo, x), lat: 4 (over y_hi, core).
Axes of the slice: x: 4, y: 4 (y_hi: 2, y_lo: 2; y = y_hi * 2 + y_lo), z: 8, core: 2. Of those that a mesh axis runs over, the one named last changes fastest.
Arguments:
- tokens: bfloat16 [2, 240, 1536, 512], P(None, 'lat', 'lon'), may hold values from -16 to 16
- land_sea: int32 [2, 240, 1536], P(None, 'lat', 'lon'), may hold values from 0 to 2
- w_qkv: bfloat16 [512, 1536], replicated, may hold values from -0.25 to 0.25
- w_out: bfloat16 [512, 512], replicated, may hold values from -0.25 to 0.25
- norm_gain: float32 [512], replicated, may hold values from 0.1 to 1.9
Outputs:
- mixed: bfloat16 [2, 240, 1536, 512], P(None, 'lat', 'lon')
All inputs are finite; a program needn't handle non-finite values.
Results may differ from a plain program's by a relative error of at most 0.006.
Values may be sent and summed in bfloat16 or wider, within the bound.
A program may use at most 192 MiB of HBM per device.

v0:
```python
import functools

import jax
import jax.numpy as jnp
import numpy as np
from jax import lax
from jax.experimental import pallas as pl
from jax.experimental.pallas import tpu as pltpu
from jax.sharding import PartitionSpec as P

HEADS = 8
HEAD = 64
WIN_LAT = 6
WIN_LON = 12
HALF_LAT = 3
HALF_LON = 6
LEV = 2
COLS = 24
D = 512
STEPS = 10
COMBOS = LEV * WIN_LAT
COUNT = COMBOS * WIN_LON
EDGE = COMBOS * HALF_LON
START = 5
AHEAD = 3
BIG = 1e30
MESH = pl.DeviceIdType.MESH
F32 = jnp.float32
BF16 = jnp.bfloat16


def centre_tokens():
    found = [(n, 8 + s) for n in range(COMBOS) for s in range(8)]
    for m in range(COMBOS // 2):
        found += [(2 * m, 16), (2 * m, 17), (2 * m + 1, 16), (2 * m + 1, 17)]
        found += [(2 * m + 1, 6), (2 * m + 1, 7), (2 * m, 6), (2 * m, 7)]
    return found


def left_tokens():
    found = []
    for n in range(9):
        k = n % 3
        found += [(n, s) for s in range(6)] + [(9 + n // 3, 2 * k), (9 + n // 3, 2 * k + 1)]
    return found


def right_tokens():
    found = []
    for n in range(9):
        k = n % 3
        found += [(9 + n // 3, 18 + 2 * k), (9 + n // 3, 19 + 2 * k)] + [(n, 16 + s) for s in range(2, 8)]
    return found


def tables():
    split = [(n, c - HALF_LON) for n, c in right_tokens()] + [(n, c + 18) for n, c in left_tokens()]
    both = [(n, c - HALF_LON) for n, c in centre_tokens()] + split
    column = np.zeros((2 * COUNT, 32), np.float32)
    lane = np.zeros((2 * COUNT, 128), np.int32)
    lower = np.zeros((2 * COUNT, 128), np.float32)
    for t, (n, c) in enumerate(both):
        level, row = divmod(n, WIN_LAT)
        column[t, c] = 1.0
        lane[t] = np.arange(128) - (64 * level + row)
        lower[t] = 3.0 if row >= HALF_LAT else 0.0
    return column.astype(jnp.bfloat16), lane, lower


def dot(a, b):
    return lax.dot_general(a, b, (((1,), (0,)), ((), ())), preferred_element_type=F32)


def dot_t(a, b):
    return lax.dot_general(a, b, (((1,), (1,)), ((), ())), preferred_element_type=F32)


def rows_of(shape):
    return lax.broadcasted_iota(jnp.int32, shape, 0)


def lanes_of(shape):
    return lax.broadcasted_iota(jnp.int32, shape, 1)


def roll(x, by):
    return pltpu.roll(x, by, 0)


def attend(q, hot, k, far, v):
    n = q.shape[0]
    first = lanes_of((n, 128)) < HEAD
    hot2 = jnp.concatenate([hot, hot], axis=0).astype(BF16)
    ones = jnp.ones((COUNT, 128), BF16)
    found = []
    for pair in range(HEADS // 2):
        cut = slice(128 * pair, 128 * pair + 128)
        part = q[:, cut] * (1.0 / HEAD**0.5)
        q2 = jnp.concatenate([jnp.where(first, part, 0.0), jnp.where(first, 0.0, part)], axis=0).astype(BF16)
        scores = dot_t(jnp.concatenate([q2, hot2], axis=1), jnp.concatenate([k[:, cut], far], axis=1))
        top = jnp.max(scores, axis=1, keepdims=True)
        expo = jnp.exp(scores - top).astype(BF16)
        summed = dot(expo, jnp.concatenate([v[:, cut], ones], axis=1))
        probs = summed[:, :128] / summed[:, 128:]
        found.append(jnp.where(first, probs[:n], probs[n:]))
    return jnp.concatenate(found, axis=1)


def finish(x, att, w_out, gain):
    proj = dot(att.astype(BF16), w_out)
    centre = proj - jnp.mean(proj, axis=1, keepdims=True)
    spread = jnp.mean(centre * centre, axis=1, keepdims=True)
    return x + gain * (centre * lax.rsqrt(spread + 1e-05))


def features(spread, lane, lower, step, edge):
    surface = jnp.sum(jnp.where(lane == WIN_LAT * step, spread, 0.0), axis=1, keepdims=True)
    same = surface + lower * edge == lanes_of((COUNT, 128)).astype(F32)
    return jnp.where(same, 1.0, 0.0), jnp.where(same, 0.0, -BIG).astype(BF16)


def fold(x):
    return jnp.concatenate([x[:, : D // 2], x[:, D // 2 :]], axis=0).astype(BF16)


def unfold(x):
    x = x.astype(F32)
    return jnp.concatenate([x[:EDGE], x[EDGE:]], axis=1)


def kernel(
    tokens, land, w_qkv, w_out, gain, column, lane, lower, out,
    xs, land_v, wq_v, wo_v, gain_v, column_v, lane_v, lower_v,
    to_west, to_east, from_west, from_east, mine, theirs, spread, centre, res,
    x_sem, x9_sem, in_sem, lat_sem, land_sem, west_send, west_recv, east_send, east_recv, out_sem, back_sem,
):
    lon, lat = lax.axis_index("lon"), lax.axis_index("lat")
    nlon, nlat = lax.axis_size("lon"), lax.axis_size("lat")
    west = (lax.rem(lon + nlon - 1, nlon), lat)
    east = (lax.rem(lon + 1, nlon), lat)
    north = (lon, lax.rem(lat + nlat - 1, nlat))
    south = (lon, lax.rem(lat + 1, nlat))
    last = jnp.where(lat == nlat - 1, 1.0, 0.0)

    barrier = pltpu.get_barrier_semaphore()
    for near in (west, east, north, south):
        pl.semaphore_signal(barrier, inc=1, device_id=near, device_id_type=MESH)

    def x_copy(a):
        return pltpu.make_async_copy(tokens.at[:, pl.ds(WIN_LAT * a + HALF_LAT, WIN_LAT)], xs.at[a], x_sem.at[a])

    x9_copy = pltpu.make_async_copy(
        tokens.at[:, WIN_LAT * STEPS - HALF_LAT : WIN_LAT * STEPS], xs.at[STEPS - 1, :, 0:HALF_LAT], x9_sem
    )
    ins = [
        pltpu.make_async_copy(src, dst, in_sem.at[i])
        for i, (src, dst) in enumerate(
            [(land, land_v), (column, column_v), (lane, lane_v), (lower, lower_v), (gain, gain_v), (w_qkv, wq_v), (w_out, wo_v)]
        )
    ]

    def remote(src, dst, send, recv, device):
        return pltpu.make_async_remote_copy(
            src_ref=src, dst_ref=dst, send_sem=send, recv_sem=recv, device_id=device, device_id_type=MESH
        )

    lat_copy = remote(tokens.at[:, 0:HALF_LAT], xs.at[STEPS - 1, :, HALF_LAT:WIN_LAT], lat_sem.at[0], lat_sem.at[1], north)
    land_copy = remote(mine, theirs, land_sem.at[0], land_sem.at[1], east)
    back_copy = remote(res.at[STEPS - 1, :, HALF_LAT:WIN_LAT], out.at[:, 0:HALF_LAT], back_sem.at[0], back_sem.at[1], south)

    def west_copy(a):
        return remote(to_west.at[a], from_east.at[a], west_send.at[a], west_recv.at[a], west)

    def east_copy(a):
        return remote(to_east.at[a], from_west.at[a], east_send.at[a], east_recv.at[a], east)

    def out_copy(a):
        return pltpu.make_async_copy(res.at[a], out.at[:, pl.ds(WIN_LAT * a + HALF_LAT, WIN_LAT)], out_sem.at[a])

    out9_copy = pltpu.make_async_copy(
        res.at[STEPS - 1, :, 0:HALF_LAT], out.at[:, WIN_LAT * STEPS - HALF_LAT : WIN_LAT * STEPS], out_sem.at[STEPS - 1]
    )

    for i in range(STEPS):
        a = (i + START) % STEPS
        if a == STEPS - 1:
            x9_copy.start()
        else:
            x_copy(a).start()
        if i == 0:
            for copy in ins:
                copy.start()
    pl.semaphore_wait(barrier, 4)
    lat_copy.start()

    row8 = rows_of((8, D))

    def tile(a, n, c):
        return xs[a, n // WIN_LAT, n % WIN_LAT, 8 * c : 8 * c + 8, :].astype(F32)

    def send(a):
        t0 = [tile(a, n, 0) for n in range(COMBOS)]
        t2 = [tile(a, n, 2) for n in range(COMBOS)]
        left = [jnp.where(row8 < 6, t0[n], roll(t0[9 + n // 3], 6 - 2 * (n % 3))) for n in range(9)]
        right = [jnp.where(row8 >= 2, t2[n], roll(t2[9 + n // 3], 6 - 2 * (n % 3))) for n in range(9)]
        to_west[a] = fold(jnp.concatenate(left, axis=0))
        to_east[a] = fold(jnp.concatenate(right, axis=0))
        west_copy(a).start()
        east_copy(a).start()

    def whole(a):
        t0 = [tile(a, n, 0) for n in range(COMBOS)]
        t2 = [tile(a, n, 2) for n in range(COMBOS)]
        parts = [tile(a, n, 1) for n in range(COMBOS)]
        for m in range(COMBOS // 2):
            low = jnp.where(row8 < 2, t2[2 * m], roll(t2[2 * m + 1], 2))
            high = jnp.where(row8 < 6, roll(t0[2 * m + 1], 6), t0[2 * m])
            parts.append(jnp.where(row8 < 4, low, high))
        x = jnp.concatenate(parts, axis=0)
        qkv = dot(x.astype(BF16), wq_v[...])
        edge = last * jnp.where(a == STEPS - 1, 1.0, 0.0)
        hot, far = features(spread[0], lane_v[:COUNT], lower_v[:COUNT], a, edge)
        att = attend(qkv[:, :D], hot, qkv[:, D : 2 * D].astype(BF16), far, qkv[:, 2 * D :].astype(BF16))
        centre[a] = finish(x, att, wo_v[...], gain_v[...]).astype(BF16)

    def split(a):
        left, right = unfold(to_west[a]), unfold(to_east[a])
        before = jnp.concatenate([unfold(from_west[a]), left], axis=0).astype(BF16)
        after = jnp.concatenate([right, unfold(from_east[a])], axis=0).astype(BF16)
        x = jnp.concatenate([left, right], axis=0)
        q = dot(x.astype(BF16), wq_v[:, :D])
        kv = dot(jnp.concatenate([before, after], axis=0), wq_v[:, D:]).astype(BF16)
        edge = last * jnp.where(a == STEPS - 1, 1.0, 0.0)
        lanes, lowers = lane_v[COUNT:], lower_v[COUNT:]
        hot0, far0 = features(spread[1], lanes, lowers, a, edge)
        hot2, far2 = features(spread[2], lanes, lowers, a, edge)
        att0 = attend(q[:EDGE], hot0[EDGE:], kv[:COUNT, :D], far0, kv[:COUNT, D:])
        att2 = attend(q[EDGE:], hot2[:EDGE], kv[COUNT:, :D], far2, kv[COUNT:, D:])
        y = finish(x, jnp.concatenate([att0, att2], axis=0), wo_v[...], gain_v[...])
        lefts = [y[8 * n : 8 * n + 8] for n in range(9)]
        rights = [y[EDGE + 8 * n : EDGE + 8 * n + 8] for n in range(9)]
        mid = centre[a].astype(F32)
        for n in range(COMBOS):
            rest = mid[96 + 8 * (n // 2) : 104 + 8 * (n // 2)]
            rest0, rest2 = (rest, rest) if n % 2 == 0 else (roll(rest, 2), roll(rest, 6))
            if n < 9:
                tile0 = jnp.where(row8 < 6, lefts[n], rest0)
                tile2 = jnp.where(row8 >= 2, rights[n], rest2)
            else:
                b = 3 * (n - 9)
                low = jnp.where(row8 < 2, roll(lefts[b], 2), roll(lefts[b + 1], 4))
                tile0 = jnp.where(row8 < 4, low, jnp.where(row8 < 6, roll(lefts[b + 2], 6), rest0))
                low = jnp.where(row8 < 2, rest2, roll(rights[b], 2))
                tile2 = jnp.where(row8 < 4, low, jnp.where(row8 < 6, roll(rights[b + 1], 4), roll(rights[b + 2], 6)))
            whole_row = jnp.concatenate([tile0, mid[8 * n : 8 * n + 8], tile2], axis=0)
            res[a, n // WIN_LAT, n % WIN_LAT] = whole_row.astype(BF16)

    def early(i, carry):
        a = i + START
        x_copy(a).wait()
        send(a)
        return carry

    lax.fori_loop(0, STEPS - 1 - START, early, 0)

    for copy in ins[:4]:
        copy.wait()
    across = jnp.zeros((COLS, 128), F32)
    rows = land_v.shape[2]
    for level in range(LEV):
        place = rows_of((rows, 128)) + 64 * level == lanes_of((rows, 128))
        across += dot(land_v[level].astype(F32).astype(BF16), jnp.where(place, 1.0, 0.0).astype(BF16))
    mine[...] = jnp.concatenate([across, jnp.zeros((32 - COLS, 128), F32)], axis=0).astype(BF16)
    land_copy.start()
    spread[0] = dot(column_v[:COUNT], mine[...])
    spread[2] = dot(column_v[COUNT:], mine[...])
    for copy in ins[4:]:
        copy.wait()

    def ahead(i, carry):
        whole(i + START)
        return carry

    lax.fori_loop(0, AHEAD, ahead, 0)
    x9_copy.wait()
    lat_copy.wait()
    send(STEPS - 1)

    def late(a, carry):
        x_copy(a).wait()
        send(a)
        return carry

    lax.fori_loop(0, START, late, 0)
    land_copy.wait()
    spread[1] = dot(column_v[COUNT:], theirs[...])

    def step(i, carry):
        a = lax.rem(i + START, STEPS)
        west_copy(a).wait()
        east_copy(a).wait()
        split(a)

        @pl.when(a == STEPS - 1)
        def _():
            back_copy.start()
            out9_copy.start()

        @pl.when(a != STEPS - 1)
        def _():
            out_copy(a).start()

        @pl.when(i < STEPS - AHEAD)
        def _():
            whole(lax.rem(i + AHEAD + START, STEPS))

        return carry

    lax.fori_loop(0, STEPS, step, 0)

    def drain(a, carry):
        out_copy(a).wait()
        return carry

    lax.fori_loop(0, STEPS - 1, drain, 0)
    out9_copy.wait()
    back_copy.wait()


def body(tokens, land_sea, w_qkv, w_out, norm_gain):
    column, lane, lower = tables()
    land_sea = jnp.transpose(land_sea, (0, 2, 1))
    anywhere = pl.BlockSpec(memory_space=pl.ANY)
    hbm = pl.BlockSpec(memory_space=pltpu.HBM)
    dma = pltpu.SemaphoreType.DMA
    vmem = pltpu.VMEM
    band = (STEPS, LEV, WIN_LAT, COLS, D)
    folded = (STEPS, COUNT, D // 2)
    return pl.pallas_call(
        kernel,
        out_shape=jax.ShapeDtypeStruct(tokens.shape, BF16),
        in_specs=[hbm] * 8,
        out_specs=anywhere,
        scratch_shapes=[
            vmem(band, BF16),
            vmem(land_sea.shape, jnp.int32),
            vmem(w_qkv.shape, BF16),
            vmem(w_out.shape, BF16),
            vmem((1, D), F32),
            vmem(column.shape, BF16),
            vmem(lane.shape, jnp.int32),
            vmem(lower.shape, F32),
            vmem(folded, BF16),
            vmem(folded, BF16),
            vmem(folded, BF16),
            vmem(folded, BF16),
            vmem((32, 128), BF16),
            vmem((32, 128), BF16),
            vmem((3, COUNT, 128), F32),
            vmem((STEPS, COUNT, D), BF16),
            vmem(band, BF16),
            dma((STEPS,)),
            dma,
            dma((7,)),
            dma((2,)),
            dma((2,)),
            dma((STEPS,)),
            dma((STEPS,)),
            dma((STEPS,)),
            dma((STEPS,)),
            dma((STEPS,)),
            dma((2,)),
        ],
        compiler_params=pltpu.CompilerParams(
            collective_id=0, has_side_effects=True, vmem_limit_bytes=63 * 1024 * 1024
        ),
    )(tokens, land_sea, w_qkv, w_out, norm_gain.reshape(1, D), column, lane, lower)


def solution(mesh):
    in_specs = (P(None, "lat", "lon", None), P(None, "lat", "lon"), P(), P(), P())
    out_specs = P(None, "lat", "lon", None)
    return jax.shard_map(body, mesh=mesh, in_specs=in_specs, out_specs=out_specs, check_vma=False)
```

profile of v0, /device:TPU:193, one launch (start us, length us, event | category | flops | bytes accessed | tf_op | source)
XLA Modules:
  0.0 53.9 jit_solution(17594242801262889055)
XLA Ops:
  0.0 50.3 %shard_map.82 = bf16[2,60,24,512]{3,2,1,0:T(8,128)(2,1)} custom-call(bf16[2,60,24,512]{3,2,1,0:T(8,128)(2,1)} %tokens.1, s32[2,24,60]{2,1,0:T(8,128)} %bitcast.2, bf16[512,1536]{1,0:T(8,128)(2,1)} %w_qkv.1, bf16[512,512]{1,0:T(8,128)(2,1)} %w_out.1, f32[1,512]{1,0:T(1,128)} %bitcast.3, bf16[288,32]{1,0:T(8,128)(2,1)} %constant.6.clone.column, ...), custom_call_target="tpu_custom_call" | custom-call | tf_op jit(solution)/shard_map/pallas_call | solution.py:339
  50.3 3.6 %copy.10 = bf16[2,60,24,512]{3,2,1,0:T(8,128)(2,1)} copy(bf16[2,60,24,512]{3,2,1,0:T(8,128)(2,1)} %shard_map.82) | data formatting | bytes 5898240
where the time goes:
time: 54 us; the launch traced here: 53.9 us
  Pallas kernels  50.3 us (93%)
  local copies, waits for them, and re-layouts  3.63 us (7%)
    pallas_call x1, Pallas kernels, body(): pl.pallas_call(kernel, out_shape=jax.ShapeDtypeStruct(tokens.shape, BF16)...  50.3 us
    unnamed x1, local copies, waits for them, and re-layouts  3.63 us

commit v1 on v0

--- a/solution.py
+++ b/solution.py
@@ -21,7 +21,7 @@
 COMBOS = LEV * WIN_LAT
 COUNT = COMBOS * WIN_LON
 EDGE = COMBOS * HALF_LON
-START = 5
+START = 2
 AHEAD = 3
 BIG = 1e30
 MESH = pl.DeviceIdType.MESH
@@ -90,19 +90,21 @@
 def attend(q, hot, k, far, v):
     n = q.shape[0]
     first = lanes_of((n, 128)) < HEAD
+    keep0 = jnp.where(lanes_of((1, 128)) < HEAD, 1.0 / HEAD**0.5, 0.0)
+    keep1 = jnp.where(lanes_of((1, 128)) < HEAD, 0.0, 1.0 / HEAD**0.5)
     hot2 = jnp.concatenate([hot, hot], axis=0).astype(BF16)
     ones = jnp.ones((COUNT, 128), BF16)
     found = []
     for pair in range(HEADS // 2):
         cut = slice(128 * pair, 128 * pair + 128)
-        part = q[:, cut] * (1.0 / HEAD**0.5)
-        q2 = jnp.concatenate([jnp.where(first, part, 0.0), jnp.where(first, 0.0, part)], axis=0).astype(BF16)
+        part = q[:, cut]
+        q2 = jnp.concatenate([part * keep0, part * keep1], axis=0).astype(BF16)
         scores = dot_t(jnp.concatenate([q2, hot2], axis=1), jnp.concatenate([k[:, cut], far], axis=1))
         top = jnp.max(scores, axis=1, keepdims=True)
         expo = jnp.exp(scores - top).astype(BF16)
         summed = dot(expo, jnp.concatenate([v[:, cut], ones], axis=1))
-        probs = summed[:, :128] / summed[:, 128:]
-        found.append(jnp.where(first, probs[:n], probs[n:]))
+        top_part = jnp.where(first, summed[:n, :128], summed[n:, :128])
+        found.append(top_part / jnp.where(first, summed[:n, 128:], summed[n:, 128:]))
     return jnp.concatenate(found, axis=1)
 
 
@@ -255,13 +257,26 @@
             whole_row = jnp.concatenate([tile0, mid[8 * n : 8 * n + 8], tile2], axis=0)
             res[a, n // WIN_LAT, n % WIN_LAT] = whole_row.astype(BF16)
 
-    def early(i, carry):
-        a = i + START
-        x_copy(a).wait()
-        send(a)
+    def both(a, b):
+        split(a)
+        whole(b)
+
+    nine = STEPS - 1 - START
+
+    nine = STEPS - 1 - START
+    calm = lon == nlon - 1
+
+    def early(i):
+        send(lax.rem(i + START, STEPS - 1))
+
+    x_copy(START).wait()
+    early(0)
+
+    def loaded(i, carry):
+        x_copy(lax.rem(i + START, STEPS - 1)).wait()
         return carry
 
-    lax.fori_loop(0, STEPS - 1 - START, early, 0)
+    lax.fori_loop(1, STEPS - 1, loaded, 0)
 
     for copy in ins[:4]:
         copy.wait()
@@ -279,27 +294,44 @@
 
     def ahead(i, carry):
         whole(i + START)
+
+        @pl.when(((i == 0) & ~calm) | ((i == 1) & calm))
+        def _():
+            early(1)
+
+        @pl.when((i == 2) & ~calm)
+        def _():
+            early(2)
+
         return carry
 
     lax.fori_loop(0, AHEAD, ahead, 0)
-    x9_copy.wait()
-    lat_copy.wait()
-    send(STEPS - 1)
-
-    def late(a, carry):
-        x_copy(a).wait()
-        send(a)
-        return carry
-
-    lax.fori_loop(0, START, late, 0)
     land_copy.wait()
     spread[1] = dot(column_v[COUNT:], theirs[...])
 
-    def step(i, carry):
+    def step(i, carry, more):
         a = lax.rem(i + START, STEPS)
+        if more:
+            @pl.when((i < nine - AHEAD) & ~calm)
+            def _():
+                early(i + AHEAD)
+
+            @pl.when((i > nine - AHEAD) | calm)
+            def _():
+                early(i + AHEAD - 1)
+
+            @pl.when(i == nine - AHEAD)
+            def _():
+                x9_copy.wait()
+                lat_copy.wait()
+                send(STEPS - 1)
+
         west_copy(a).wait()
         east_copy(a).wait()
-        split(a)
+        if more:
+            both(a, lax.rem(i + AHEAD + START, STEPS))
+        else:
+            split(a)
 
         @pl.when(a == STEPS - 1)
         def _():
@@ -310,13 +342,10 @@
         def _():
             out_copy(a).start()
 
-        @pl.when(i < STEPS - AHEAD)
-        def _():
-            whole(lax.rem(i + AHEAD + START, STEPS))
-
         return carry
 
-    lax.fori_loop(0, STEPS, step, 0)
+    lax.fori_loop(0, STEPS - AHEAD, functools.partial(step, more=True), 0)
+    lax.fori_loop(STEPS - AHEAD, STEPS, functools.partial(step, more=False), 0)
 
     def drain(a, carry):
         out_copy(a).wait()
@@ -331,7 +360,7 @@
     column, lane, lower = tables()
     land_sea = jnp.transpose(land_sea, (0, 2, 1))
     anywhere = pl.BlockSpec(memory_space=pl.ANY)
-    hbm = pl.BlockSpec(memory_space=pltpu.HBM)
+    operands = (tokens, land_sea, w_qkv, w_out, norm_gain.reshape(1, D), column, lane, lower)
     dma = pltpu.SemaphoreType.DMA
     vmem = pltpu.VMEM
     band = (STEPS, LEV, WIN_LAT, COLS, D)
@@ -339,7 +368,7 @@
     return pl.pallas_call(
         kernel,
         out_shape=jax.ShapeDtypeStruct(tokens.shape, BF16),
-        in_specs=[hbm] * 8,
+        in_specs=[anywhere] * 8,
         out_specs=anywhere,
         scratch_shapes=[
             vmem(band, BF16),
@@ -372,9 +401,9 @@
             dma((2,)),
         ],
         compiler_params=pltpu.CompilerParams(
-            collective_id=0, has_side_effects=True, vmem_limit_bytes=63 * 1024 * 1024
+            collective_id=0, has_side_effects=True, vmem_limit_bytes=48 * 1024 * 1024
         ),
-    )(tokens, land_sea, w_qkv, w_out, norm_gain.reshape(1, D), column, lane, lower)
+    )(*[pltpu.with_memory_space_constraint(x, pltpu.HBM) for x in operands])
 
 
 def solution(mesh):

time: 54 us -> 40 us (0.74)
  the two profiles are of different devices: /device:TPU:193 before, /device:TPU:1 now
where the time goes in v1:
time: 40 us; the launch traced here: 39.9 us
  Pallas kernels  38.3 us (96%)
  local copies, waits for them, and re-layouts  1.6 us (4%)
    pallas_call x1, Pallas kernels, body(): pl.pallas_call(kernel, out_shape=jax.ShapeDtypeStruct(tokens.shape, BF16)...  38.3 us
    unnamed x1, local copies, waits for them, and re-layouts  1.6 us

profile of v1, /device:TPU:1, one launch (start us, length us, event | category | flops | bytes accessed | tf_op | source)
XLA Modules:
  0.0 39.9 jit_solution(17563872707894086686)
XLA Ops:
  0.0 38.3 %shard_map.82 = bf16[2,60,24,512]{3,2,1,0:T(8,128)(2,1)S(1)} custom-call(bf16[2,60,24,512]{3,2,1,0:T(8,128)(2,1)} %tokens.1, s32[2,24,60]{2,1,0:T(8,128)} %bitcast.2, bf16[512,1536]{1,0:T(8,128)(2,1)} %w_qkv.1, bf16[512,512]{1,0:T(8,128)(2,1)} %w_out.1, f32[1,512]{1,0:T(1,128)} %bitcast.3, bf16[288,32]{1,0:T(8,128)(2,1)} %constant.6.clone.column, ...), custom_call_target="tpu_custom_call" | custom-call | tf_op jit(solution)/shard_map/pallas_call | solution.py:368
  38.3 1.6 %copy.10 = bf16[2,60,24,512]{3,2,1,0:T(8,128)(2,1)} copy(bf16[2,60,24,512]{3,2,1,0:T(8,128)(2,1)S(1)} %shard_map.82) | data formatting | bytes 5898240

commit v2 on v1

--- a/solution.py
+++ b/solution.py
@@ -21,8 +21,9 @@
 COMBOS = LEV * WIN_LAT
 COUNT = COMBOS * WIN_LON
 EDGE = COMBOS * HALF_LON
-START = 2
-AHEAD = 3
+START = 0
+AHEAD = 2
+RATE = 3
 BIG = 1e30
 MESH = pl.DeviceIdType.MESH
 F32 = jnp.float32
@@ -210,7 +211,7 @@
         west_copy(a).start()
         east_copy(a).start()
 
-    def whole(a):
+    def centre_x(a):
         t0 = [tile(a, n, 0) for n in range(COMBOS)]
         t2 = [tile(a, n, 2) for n in range(COMBOS)]
         parts = [tile(a, n, 1) for n in range(COMBOS)]
@@ -218,27 +219,45 @@
             low = jnp.where(row8 < 2, t2[2 * m], roll(t2[2 * m + 1], 2))
             high = jnp.where(row8 < 6, roll(t0[2 * m + 1], 6), t0[2 * m])
             parts.append(jnp.where(row8 < 4, low, high))
-        x = jnp.concatenate(parts, axis=0)
+        return jnp.concatenate(parts, axis=0)
+
+    def whole(*bands):
+        x = jnp.concatenate([centre_x(a) for a in bands], axis=0)
         qkv = dot(x.astype(BF16), wq_v[...])
-        edge = last * jnp.where(a == STEPS - 1, 1.0, 0.0)
-        hot, far = features(spread[0], lane_v[:COUNT], lower_v[:COUNT], a, edge)
-        att = attend(qkv[:, :D], hot, qkv[:, D : 2 * D].astype(BF16), far, qkv[:, 2 * D :].astype(BF16))
-        centre[a] = finish(x, att, wo_v[...], gain_v[...]).astype(BF16)
-
-    def split(a):
-        left, right = unfold(to_west[a]), unfold(to_east[a])
-        before = jnp.concatenate([unfold(from_west[a]), left], axis=0).astype(BF16)
-        after = jnp.concatenate([right, unfold(from_east[a])], axis=0).astype(BF16)
-        x = jnp.concatenate([left, right], axis=0)
+        att = []
+        for d, a in enumerate(bands):
+            part = qkv[COUNT * d : COUNT * d + COUNT]
+            edge = last * jnp.where(a == STEPS - 1, 1.0, 0.0)
+            hot, far = features(spread[0], lane_v[:COUNT], lower_v[:COUNT], a, edge)
+            att.append(attend(part[:, :D], hot, part[:, D : 2 * D].astype(BF16), far, part[:, 2 * D :].astype(BF16)))
+        y = finish(x, jnp.concatenate(att, axis=0), wo_v[...], gain_v[...]).astype(BF16)
+        for d, a in enumerate(bands):
+            centre[a] = y[COUNT * d : COUNT * d + COUNT]
+
+    def split(*bands):
+        own, keys = [], []
+        for a in bands:
+            left, right = unfold(to_west[a]), unfold(to_east[a])
+            keys.append(jnp.concatenate([unfold(from_west[a]), left], axis=0).astype(BF16))
+            keys.append(jnp.concatenate([right, unfold(from_east[a])], axis=0).astype(BF16))
+            own += [left, right]
+        x = jnp.concatenate(own, axis=0)
         q = dot(x.astype(BF16), wq_v[:, :D])
-        kv = dot(jnp.concatenate([before, after], axis=0), wq_v[:, D:]).astype(BF16)
-        edge = last * jnp.where(a == STEPS - 1, 1.0, 0.0)
+        kv = dot(jnp.concatenate(keys, axis=0), wq_v[:, D:]).astype(BF16)
         lanes, lowers = lane_v[COUNT:], lower_v[COUNT:]
-        hot0, far0 = features(spread[1], lanes, lowers, a, edge)
-        hot2, far2 = features(spread[2], lanes, lowers, a, edge)
-        att0 = attend(q[:EDGE], hot0[EDGE:], kv[:COUNT, :D], far0, kv[:COUNT, D:])
-        att2 = attend(q[EDGE:], hot2[:EDGE], kv[COUNT:, :D], far2, kv[COUNT:, D:])
-        y = finish(x, jnp.concatenate([att0, att2], axis=0), wo_v[...], gain_v[...])
+        att = []
+        for d, a in enumerate(bands):
+            edge = last * jnp.where(a == STEPS - 1, 1.0, 0.0)
+            for w in range(2):
+                hot, far = features(spread[1 + w], lanes, lowers, a, edge)
+                hot = hot[EDGE:] if w == 0 else hot[:EDGE]
+                part = kv[COUNT * (2 * d + w) : COUNT * (2 * d + w + 1)]
+                att.append(attend(q[EDGE * (2 * d + w) : EDGE * (2 * d + w + 1)], hot, part[:, :D], far, part[:, D:]))
+        y = finish(x, jnp.concatenate(att, axis=0), wo_v[...], gain_v[...])
+        for d, a in enumerate(bands):
+            assemble(a, y[COUNT * d : COUNT * d + COUNT])
+
+    def assemble(a, y):
         lefts = [y[8 * n : 8 * n + 8] for n in range(9)]
         rights = [y[EDGE + 8 * n : EDGE + 8 * n + 8] for n in range(9)]
         mid = centre[a].astype(F32)
@@ -257,26 +276,20 @@
             whole_row = jnp.concatenate([tile0, mid[8 * n : 8 * n + 8], tile2], axis=0)
             res[a, n // WIN_LAT, n % WIN_LAT] = whole_row.astype(BF16)
 
-    def both(a, b):
-        split(a)
-        whole(b)
-
-    nine = STEPS - 1 - START
-
-    nine = STEPS - 1 - START
-    calm = lon == nlon - 1
+    nine = (STEPS - 1 - START) // 2
 
     def early(i):
         send(lax.rem(i + START, STEPS - 1))
 
-    x_copy(START).wait()
-    early(0)
+    for d in range(2):
+        x_copy(d + START).wait()
+        early(d)
 
     def loaded(i, carry):
         x_copy(lax.rem(i + START, STEPS - 1)).wait()
         return carry
 
-    lax.fori_loop(1, STEPS - 1, loaded, 0)
+    lax.fori_loop(2, STEPS - 1, loaded, 0)
 
     for copy in ins[:4]:
         copy.wait()
@@ -292,16 +305,22 @@
     for copy in ins[4:]:
         copy.wait()
 
+    def pair(i):
+        return [lax.rem(2 * i + d + START, STEPS) for d in range(2)]
+
+    def more_sends(slot):
+        for d in range(RATE):
+
+            @pl.when(2 + RATE * slot + d < STEPS - 1)
+            def _():
+                early(2 + RATE * slot + d)
+
     def ahead(i, carry):
-        whole(i + START)
-
-        @pl.when(((i == 0) & ~calm) | ((i == 1) & calm))
+        whole(*pair(i))
+
+        @pl.when(i < AHEAD - 1)
         def _():
-            early(1)
-
-        @pl.when((i == 2) & ~calm)
-        def _():
-            early(2)
+            more_sends(i)
 
         return carry
 
@@ -309,43 +328,40 @@
     land_copy.wait()
     spread[1] = dot(column_v[COUNT:], theirs[...])
 
-    def step(i, carry, more):
-        a = lax.rem(i + START, STEPS)
-        if more:
-            @pl.when((i < nine - AHEAD) & ~calm)
-            def _():
-                early(i + AHEAD)
-
-            @pl.when((i > nine - AHEAD) | calm)
-            def _():
-                early(i + AHEAD - 1)
-
-            @pl.when(i == nine - AHEAD)
+    def step(i, carry, merged):
+        more_sends(i + AHEAD - 1)
+        if merged == 1:
+
+            @pl.when(i == nine - 1)
             def _():
                 x9_copy.wait()
                 lat_copy.wait()
                 send(STEPS - 1)
 
-        west_copy(a).wait()
-        east_copy(a).wait()
-        if more:
-            both(a, lax.rem(i + AHEAD + START, STEPS))
-        else:
-            split(a)
-
-        @pl.when(a == STEPS - 1)
-        def _():
-            back_copy.start()
-            out9_copy.start()
-
-        @pl.when(a != STEPS - 1)
-        def _():
-            out_copy(a).start()
+        bands = pair(i)
+        for a in bands:
+            west_copy(a).wait()
+            east_copy(a).wait()
+        split(*bands)
+        if merged:
+            whole(*pair(i + merged))
+        for a in bands:
+
+            @pl.when(a == STEPS - 1)
+            def _():
+                back_copy.start()
+                out9_copy.start()
+
+            @pl.when(a != STEPS - 1)
+            def _():
+                out_copy(a).start()
 
         return carry
 
-    lax.fori_loop(0, STEPS - AHEAD, functools.partial(step, more=True), 0)
-    lax.fori_loop(STEPS - AHEAD, STEPS, functools.partial(step, more=False), 0)
+    lax.fori_loop(0, nine - AHEAD, functools.partial(step, merged=AHEAD), 0)
+    lax.fori_loop(nine - AHEAD, nine - 1, functools.partial(step, merged=0), 0)
+    lax.fori_loop(nine - 1, nine, functools.partial(step, merged=1), 0)
+    lax.fori_loop(nine, STEPS // 2, functools.partial(step, merged=0), 0)
 
     def drain(a, carry):
         out_copy(a).wait()

time: 40 us -> 39.5 us (0.988)
  Pallas kernels: 38.3 us -> 37.8 us
    pallas_call x1, Pallas kernels: 38.3 us -> 37.8 us  [body(): pl.pallas_call(kernel, out_shape=jax.ShapeDtypeStruct(tokens.shape, BF16)...]
where the time goes in v2:
time: 39.5 us; the launch traced here: 39.4 us
  Pallas kernels  37.8 us (96%)
  local copies, waits for them, and re-layouts  1.6 us (4%)
    pallas_call x1, Pallas kernels, body(): pl.pallas_call(kernel, out_shape=jax.ShapeDtypeStruct(tokens.shape, BF16)...  37.8 us
    unnamed x1, local copies, waits for them, and re-layouts  1.6 us

profile of v2, /device:TPU:1, one launch (start us, length us, event | category | flops | bytes accessed | tf_op | source)
XLA Modules:
  0.0 39.4 jit_solution(6242264718120195412)
XLA Ops:
  0.0 37.8 %shard_map.82 = bf16[2,60,24,512]{3,2,1,0:T(8,128)(2,1)S(1)} custom-call(bf16[2,60,24,512]{3,2,1,0:T(8,128)(2,1)} %tokens.1, s32[2,24,60]{2,1,0:T(8,128)} %bitcast.2, bf16[512,1536]{1,0:T(8,128)(2,1)} %w_qkv.1, bf16[512,512]{1,0:T(8,128)(2,1)} %w_out.1, f32[1,512]{1,0:T(1,128)} %bitcast.3, bf16[288,32]{1,0:T(8,128)(2,1)} %constant.6.clone.column, ...), custom_call_target="tpu_custom_call" | custom-call | tf_op jit(solution)/shard_map/pallas_call | solution.py:384
  37.8 1.6 %copy.10 = bf16[2,60,24,512]{3,2,1,0:T(8,128)(2,1)} copy(bf16[2,60,24,512]{3,2,1,0:T(8,128)(2,1)S(1)} %shard_map.82) | data formatting | bytes 5898240

commit v3 on v2

--- a/solution.py
+++ b/solution.py
@@ -24,6 +24,8 @@
 START = 0
 AHEAD = 2
 RATE = 3
+RING = 4
+HOLD = 1
 BIG = 1e30
 MESH = pl.DeviceIdType.MESH
 F32 = jnp.float32
@@ -197,6 +199,8 @@
     lat_copy.start()
 
     row8 = rows_of((8, D))
+    hold_east = lax.rem(lon, 2 * RING) == RING - 1
+    hold_west = lax.rem(lon, 2 * RING) == RING
 
     def tile(a, n, c):
         return xs[a, n // WIN_LAT, n % WIN_LAT, 8 * c : 8 * c + 8, :].astype(F32)
@@ -208,8 +212,15 @@
         right = [jnp.where(row8 >= 2, t2[n], roll(t2[9 + n // 3], 6 - 2 * (n % 3))) for n in range(9)]
         to_west[a] = fold(jnp.concatenate(left, axis=0))
         to_east[a] = fold(jnp.concatenate(right, axis=0))
-        west_copy(a).start()
-        east_copy(a).start()
+        at_once = a == STEPS - 1
+
+        @pl.when(at_once | ~hold_west)
+        def _():
+            west_copy(a).start()
+
+        @pl.when(at_once | ~hold_east)
+        def _():
+            east_copy(a).start()
 
     def centre_x(a):
         t0 = [tile(a, n, 0) for n in range(COMBOS)]
@@ -315,6 +326,17 @@
             def _():
                 early(2 + RATE * slot + d)
 
+        for d in range(RATE):
+            a = 2 + RATE * (slot - HOLD) + d
+
+            @pl.when((a >= 0) & (a < STEPS - 1) & hold_west)
+            def _():
+                west_copy(a).start()
+
+            @pl.when((a >= 0) & (a < STEPS - 1) & hold_east)
+            def _():
+                east_copy(a).start()
+
     def ahead(i, carry):
         whole(*pair(i))
 
@@ -330,9 +352,9 @@
 
     def step(i, carry, merged):
         more_sends(i + AHEAD - 1)
-        if merged == 1:
-
-            @pl.when(i == nine - 1)
+        if merged == 0:
+
+            @pl.when(i == nine - 2)
             def _():
                 x9_copy.wait()
                 lat_copy.wait()
@@ -340,8 +362,8 @@
 
         bands = pair(i)
         for a in bands:
-            west_copy(a).wait()
-            east_copy(a).wait()
+            west_copy(a).wait_recv()
+            east_copy(a).wait_recv()
         split(*bands)
         if merged:
             whole(*pair(i + merged))
@@ -362,6 +384,13 @@
     lax.fori_loop(nine - AHEAD, nine - 1, functools.partial(step, merged=0), 0)
     lax.fori_loop(nine - 1, nine, functools.partial(step, merged=1), 0)
     lax.fori_loop(nine, STEPS // 2, functools.partial(step, merged=0), 0)
+
+    def sent(a, carry):
+        west_copy(a).wait_send()
+        east_copy(a).wait_send()
+        return carry
+
+    lax.fori_loop(0, STEPS, sent, 0)
 
     def drain(a, carry):
         out_copy(a).wait()

time: 39.5 us -> 41.3 us (1.046)
  the two profiles are of different devices: /device:TPU:1 before, /device:TPU:0 now
where the time goes in v3:
time: 41.3 us; the launch traced here: 41.2 us
  Pallas kernels  39.6 us (96%)
  local copies, waits for them, and re-layouts  1.6 us (4%)
    pallas_call x1, Pallas kernels, body(): pl.pallas_call(kernel, out_shape=jax.ShapeDtypeStruct(tokens.shape, BF16)...  39.6 us
    unnamed x1, local copies, waits for them, and re-layouts  1.6 us

profile of v3, /device:TPU:0, one launch (start us, length us, event | category | flops | bytes accessed | tf_op | source)
XLA Modules:
  0.0 41.2 jit_solution(9111226856310465125)
XLA Ops:
  0.0 39.6 %shard_map.82 = bf16[2,60,24,512]{3,2,1,0:T(8,128)(2,1)S(1)} custom-call(bf16[2,60,24,512]{3,2,1,0:T(8,128)(2,1)} %tokens.1, s32[2,24,60]{2,1,0:T(8,128)} %bitcast.2, bf16[512,1536]{1,0:T(8,128)(2,1)} %w_qkv.1, bf16[512,512]{1,0:T(8,128)(2,1)} %w_out.1, f32[1,512]{1,0:T(1,128)} %bitcast.3, bf16[288,32]{1,0:T(8,128)(2,1)} %constant.6.clone.column, ...), custom_call_target="tpu_custom_call" | custom-call | tf_op jit(solution)/shard_map/pallas_call | solution.py:413
  39.6 1.6 %copy.10 = bf16[2,60,24,512]{3,2,1,0:T(8,128)(2,1)} copy(bf16[2,60,24,512]{3,2,1,0:T(8,128)(2,1)S(1)} %shard_map.82) | data formatting | bytes 5898240
